TPU v7x, 32 devices: a whole 2x2x4 slice. The times are simulated.
32 devices in a mesh: holes: 2 (over x), depth: 16 (over z, y, core).
Axes of the slice: x: 2, y: 2, z: 4, core: 2. Of those that a mesh axis runs over, the one named last changes fastest.
Arguments:
- spectra: bfloat16 [288, 262144], P(None, ('holes', 'depth')), parts along dimension 1, may hold values from 0 to 100, as said below
- basis: bfloat16 [288, 256], replicated, may hold values from 0.099609375 to 1
- abundance: bfloat16 [256, 262144], P(None, ('holes', 'depth')), parts along dimension 1, may hold values from 0.049804688 to 1
- support: int32 [256, 2048], P(None, ('holes', 'depth')), parts along dimension 1, may hold values from 0 to 1, as said below
Outputs:
- basis_next: bfloat16 [576, 256], P('holes'), parts along dimension 0
- abundance_next: bfloat16 [256, 262144], P(None, ('holes', 'depth')), parts along dimension 1
There are 2 independent parts, one for each index of `holes`. A program takes and returns all parts, laid end to end along the dimension named above; an argument that names none is the same for every part. Nothing has to cross between parts.
Inputs may be any that keep to these rules, and one draw needn't show every extreme that they name: `support`: every component is allowed in at least one block; block densities vary from block to block. `spectra`: Nonnegative.
All inputs are finite; a program needn't handle non-finite values.
Results may differ from a plain program's by a relative error of at most 0.0016.
Values may be sent and summed in bfloat16 or wider, within the bound.
A program may use at most 128 MiB of HBM per device.

v0:
```python
import jax
import jax.numpy as jnp
from jax import lax
from jax.sharding import PartitionSpec as P

BLOCK = 128


smooth_weight = 3000.0
sparsity = 100.0


def extended(block, sides, width):
    for axis, dim in sides:
        count = lax.axis_size(axis)
        forward = [(i, i + 1) for i in range(count - 1)]
        backward = [(target, source) for source, target in forward]
        low = lax.ppermute(
            lax.slice_in_dim(block, block.shape[dim] - width, None, axis=dim), axis, forward
        )
        high = lax.ppermute(lax.slice_in_dim(block, 0, width, axis=dim), axis, backward)
        block = jnp.concatenate([low, block, high], axis=dim)
    return block


def local(spectra, basis, abundance, support):
    project = jnp.dot(basis.T, spectra, preferred_element_type=jnp.float32)
    gram_basis = jnp.dot(basis.T, basis, preferred_element_type=jnp.float32).astype(jnp.bfloat16)
    image = jnp.dot(gram_basis, abundance, preferred_element_type=jnp.float32)
    padded = extended(abundance, (("depth", 1),), 1)
    centre_f = abundance.astype(jnp.float32)
    beside = padded[:, :-2].astype(jnp.float32) + padded[:, 2:].astype(jnp.float32)
    active = jnp.repeat(support.astype(jnp.float32), BLOCK, axis=1)
    abundance_next = (
        active
        * centre_f
        * (project + smooth_weight * beside)
        / (image + 2.0 * smooth_weight * centre_f + sparsity)
    ).astype(jnp.bfloat16)
    cross = jnp.dot(spectra, abundance_next.T, preferred_element_type=jnp.float32)
    gram_abund = jnp.dot(abundance_next, abundance_next.T, preferred_element_type=jnp.float32)
    basis_f = basis.astype(jnp.float32)
    cross_all, gram_all = lax.psum((cross, gram_abund), "depth")
    lower = jnp.dot(basis_f, gram_all, precision=lax.Precision.HIGHEST)
    basis_next = (basis_f * cross_all / lower).astype(jnp.bfloat16)
    return (basis_next, abundance_next)


def solution(mesh):
    placed = (
        P(None, ("holes", "depth")),
        P(),
        P(None, ("holes", "depth")),
        P(None, ("holes", "depth")),
    )
    return jax.shard_map(
        local,
        mesh=mesh,
        in_specs=placed,
        out_specs=(P("holes", None), P(None, ("holes", "depth"))),
        check_vma=False,
    )
```

profile of v0, /device:TPU:0, one launch (start us, length us, event | category | flops | bytes accessed | tf_op | source)
XLA Modules:
  0.0 162.4 jit_solution(8115654910635306140)
XLA Ops:
  7.2 0.0 copy-start.1
  7.2 0.0 all-reduce.3.cloned.1.call-start
  7.2 1.0 fusion.6
  8.2 2.4 %collective-permute-start = (bf16[256,1]{1,0:T(8,128)(2,1)S(1)}, bf16[256,1]{1,0:T(8,128)(2,1)S(1)}, u32[]{:S(2)}, u32[]{:S(2)}) collective-permute-start(bf16[256,1]{1,0:T(8,128)(2,1)S(1)} %get-tuple-element.4), channel_id=1, source_target_pairs={{0,1},{1,2},{2,3},{3,4},{4,5},{5,6},{6,7},{7,8},{8,9},{9,10},{10,1... | collective-permute-start | bytes 1544 | tf_op jit(solution)/shard_map/ppermute | solution.py:18
  10.6 0.0 copy-start
  10.6 1.4 collective-permute-start.1
  12.0 8.0 %fusion.7 = f32[256,8192]{1,0:T(8,128)} fusion(bf16[288,256]{1,0:T(8,128)(2,1)} %param.5, bf16[288,8192]{1,0:T(8,128)(2,1)} %param.4), kind=kOutput, calls=%fused_computation.15 | convolution fusion | flops 1207959552 | bytes 13254656 | tf_op jit(solution)/shard_map/dot_general | solution.py:27
  20.0 0.0 copy-done.1
  20.0 0.1 copy.6
  20.1 0.0 collective-permute-done
  20.1 0.0 collective-permute-done.1
  20.2 4.6 %broadcast_in_dim.3 = f32[256,64,128]{2,1,0:T(8,128)} broadcast(f32[256,64]{1,0:T(8,128)S(1)} %copy.6), dimensions={0,1} | broadcast | bytes 8454144 | tf_op jit(solution)/shard_map/broadcast_in_dim | solution.py:33
  24.7 0.0 copy-done
  24.7 23.2 %fusion.3 = bf16[256,8192]{1,0:T(8,128)(2,1)} fusion(bf16[256,8192]{1,0:T(8,128)(2,1)} %param.6, f32[32,8,64,128]{3,2,1,0:T(8,128)} %bitcast.22, f32[256,8192]{1,0:T(8,128)} %fusion.7, bf16[256,1]{1,0:T(8,128)(2,1)S(1)} %collective-permute-done.1, bf16[256,1]{1,0:T(8,128)(2,1)S(1)} %collective-permute-done, bf16[288,256]{1,0:T(8,128)(2,1)S(1)} %copy-done), kind=kOutput, calls=%fused_computation.6 | convolution fusion | flops 1151401984 | bytes 25314304 | tf_op jit(solution)/shard_map/dot_general | solution.py:29
  47.9 0.0 copy-start.2
  47.9 5.6 %fusion.8 = f32[256,256]{1,0:T(8,128)} fusion(bf16[256,8192]{1,0:T(8,128)(2,1)} %fusion.3), kind=kOutput, calls=%fused_computation.16 | convolution fusion | flops 1073741824 | bytes 4456448 | tf_op jit(solution)/shard_map/dot_general | solution.py:41
  53.5 0.0 copy-done.2
  53.5 4.5 %convolution_bitcast_fusion.1 = f32[288,256]{1,0:T(8,128)} fusion(bf16[256,8192]{1,0:T(8,128)(2,1)S(1)} %copy-done.2, bf16[288,8192]{1,0:T(8,128)(2,1)} %param.4), kind=kOutput, calls=%fused_computation.11 | convolution fusion | flops 1207959552 | bytes 9207808 | tf_op jit(solution)/shard_map/dot_general | solution.py:40
  58.0 0.0 all-reduce.3.cloned.1.call-update
  58.0 95.5 %all-reduce.3.cloned.1.call-done = (f32[256,256]{1,0:T(8,128)}, f32[288,256]{1,0:T(8,128)}) async-done(((f32[256,256]{1,0:T(8,128)}, f32[288,256]{1,0:T(8,128)}), (f32[256,256]{1,0:T(8,128)}, f32[288,256]{1,0:T(8,128)})) %all-reduce.3.cloned.1.call-update) | async-done | bytes 557072 | tf_op jit(solution)/shard_map/psum | solution.py:43
  153.5 2.0 %fusion.5 = bf16[288,256]{1,0:T(8,128)(2,1)} fusion(f32[256,256]{1,0:T(8,128)} %get-tuple-element.2, bf16[288,256]{1,0:T(8,128)(2,1)S(1)} %copy-done, f32[288,256]{1,0:T(8,128)} %get-tuple-element.3), kind=kOutput, calls=%fused_computation.12 | convolution fusion | flops 226787328 | bytes 851968 | tf_op jit(solution)/shard_map/dot_general | solution.py:44
  (1 shorter events, 0.0 us)
Async XLA Ops:
  7.2 12.9 %copy-start.1 = (s32[256,64]{0,1:T(8,128)S(1)}, s32[256,64]{0,1:T(8,128)}, u32[]{:S(2)}) copy-start(s32[256,64]{0,1:T(8,128)} %param.7) | copy-start | bytes 196612
  7.2 146.4 %all-reduce.3.cloned.1.call-start = ((), (), s32[]{:S(2)}) async-start(), calls=%async_computation | async-start | bytes 1114112 | tf_op jit(solution)/shard_map/psum | solution.py:43
  8.2 12.0 %collective-permute-start = (bf16[256,1]{1,0:T(8,128)(2,1)S(1)}, bf16[256,1]{1,0:T(8,128)(2,1)S(1)}, u32[]{:S(2)}, u32[]{:S(2)}) collective-permute-start(bf16[256,1]{1,0:T(8,128)(2,1)S(1)} %get-tuple-element.4), channel_id=1, source_target_pairs={{0,1},{1,2},{2,3},{3,4},{4,5},{5,6},{6,7},{7,8},{8,9},{9,10},{10,1... | collective-permute-start | bytes 1544 | tf_op jit(solution)/shard_map/ppermute | solution.py:18
  10.6 14.2 %copy-start = (bf16[288,256]{1,0:T(8,128)(2,1)S(1)}, bf16[288,256]{1,0:T(8,128)(2,1)}, u32[]{:S(2)}) copy-start(bf16[288,256]{1,0:T(8,128)(2,1)} %param.5) | copy-start | bytes 442372
  10.6 9.6 %collective-permute-start.1 = (bf16[256,1]{1,0:T(8,128)(2,1)S(1)}, bf16[256,1]{1,0:T(8,128)(2,1)S(1)}, u32[]{:S(2)}, u32[]{:S(2)}) collective-permute-start(bf16[256,1]{1,0:T(8,128)(2,1)S(1)} %get-tuple-element.5), channel_id=1, source_target_pairs={{1,0},{2,1},{3,2},{4,3},{5,4},{6,5},{7,6},{8,7},{9,8},{10,9},{11,1... | collective-permute-start | bytes 1544 | tf_op jit(solution)/shard_map/ppermute | solution.py:21
  47.9 5.6 %copy-start.2 = (bf16[256,8192]{1,0:T(8,128)(2,1)S(1)}, bf16[256,8192]{1,0:T(8,128)(2,1)}, u32[]{:S(2)}) copy-start(bf16[256,8192]{1,0:T(8,128)(2,1)} %fusion.3) | copy-start | bytes 12582916
Sparse Core Ops, SparseCore 0:
  58.1 95.3 all-reduce.2
where the time goes:
time: 163 us; the launch traced here: 162 us
  waiting for transfers between devices  95.5 us (59%)
  matrix products  43.3 us (27%)
  between operations  14.1 us (9%)
  local copies, waits for them, and re-layouts  5.63 us (3%)
  starting transfers between devices  3.82 us (2%)
    psum x1, waiting for transfers between devices, local(): cross_all, gram_all = lax.psum((cross, gram_abund), 'depth')  95.5 us
    dot_general x1, matrix products, local(): image = jnp.dot(gram_basis, abundance, preferred_element_type=jnp.float32)  23.2 us
    dot_general x1, matrix products, local(): project = jnp.dot(basis.T, spectra, preferred_element_type=jnp.float32)  8.03 us
    dot_general x1, matrix products, local(): jnp.dot(abundance_next, abundance_next.T, preferred_element_type=jnp.floa...  5.59 us
    broadcast_in_dim x1, local copies, waits for them, and re-layouts, local(): active = jnp.repeat(support.astype(jnp.float32), BLOCK, axis=1)  4.56 us
    dot_general x1, matrix products, local(): jnp.dot(spectra, abundance_next.T, preferred_element_type=jnp.float32)  4.47 us
  transfers between devices with their start and end apart: 3, of which 1 were waited for; matrix products, arithmetic and copies ran while one was open for 5% of the time, Pallas kernels for 0%

commit v1 on v0

v1 whole, which is shorter than its diff:
```python
import functools

import jax
import jax.numpy as jnp
from jax import lax
from jax.experimental import pallas as pl
from jax.experimental.pallas import tpu as pltpu
from jax.sharding import PartitionSpec as P

BLOCK = 128
TILE = 1024
CHUNK = 256
ROWS = 64
NT = (((1,), (1,)), ((), ()))

smooth_weight = 3000.0
sparsity = 100.0


def dot(a, b):
    return jnp.dot(a, b, preferred_element_type=jnp.float32)


def dot_nt(a, b):
    return lax.dot_general(a, b, NT, preferred_element_type=jnp.float32)


def kernel(
    n, sp_hbm, basis_ref, ab_hbm, sup_ref, bn_ref, an_hbm,
    sp_v, ab_v, an_v, sup_v, bt_v, gb_v, acc, half_in, send_v, recv_v, back_v,
    sp_sem, ab_sem, an_sem, halo_s, halo_r, half_s, half_r, red_s, red_r, gat_s, gat_r, fwd_s, fwd_r,
):
    bands, pixels = sp_hbm.shape
    comps = ab_hbm.shape[0]
    tiles = pixels // TILE
    per = TILE // BLOCK
    chips = n // 2
    owners = min(chips, 8)
    stride = chips // owners
    half = comps // 2
    rows = half // owners
    gram_at = acc.shape[1] - comps

    me = lax.axis_index("depth")
    core = lax.rem(me, 2)
    chip = lax.div(me, 2)
    partner = me + 1 - 2 * core

    def load_ab(t):
        return pltpu.make_async_copy(
            ab_hbm.at[:, pl.ds(pl.multiple_of(t * TILE, TILE), TILE)],
            ab_v.at[:, pl.ds(pl.multiple_of(BLOCK + t * TILE, BLOCK), TILE)],
            ab_sem.at[t],
        )

    def load_sp(t):
        where = pl.ds(pl.multiple_of(t * TILE, TILE), TILE)
        return pltpu.make_async_copy(sp_hbm.at[:, where], sp_v.at[:, where], sp_sem.at[t])

    def store_an(t):
        where = pl.ds(pl.multiple_of(t * TILE, TILE), TILE)
        return pltpu.make_async_copy(an_v.at[:, where], an_hbm.at[:, where], an_sem.at[t])

    load_ab(0).start()
    load_ab(1).start()
    load_sp(1).start()
    for t in range(2, tiles):
        load_ab(t).start()
        load_sp(t).start()
    load_sp(0).start()

    barrier = pltpu.get_barrier_semaphore()
    for off in range(1, n):
        pl.semaphore_signal(
            barrier, inc=1, device_id={"depth": lax.rem(me + off, n)}, device_id_type=pl.DeviceIdType.MESH
        )

    to_right = pltpu.make_async_remote_copy(
        src_ref=ab_hbm.at[:, pixels - BLOCK :], dst_ref=ab_v.at[:, :BLOCK],
        send_sem=halo_s.at[0], recv_sem=halo_r.at[0],
        device_id={"depth": lax.rem(me + 1, n)}, device_id_type=pl.DeviceIdType.MESH,
    )
    to_left = pltpu.make_async_remote_copy(
        src_ref=ab_hbm.at[:, :BLOCK], dst_ref=ab_v.at[:, BLOCK + pixels :],
        send_sem=halo_s.at[1], recv_sem=halo_r.at[1],
        device_id={"depth": lax.rem(me + n - 1, n)}, device_id_type=pl.DeviceIdType.MESH,
    )

    basis = basis_ref[...]
    eye = (
        lax.broadcasted_iota(jnp.int32, (comps, comps), 0) == lax.broadcasted_iota(jnp.int32, (comps, comps), 1)
    ).astype(jnp.bfloat16)
    basis_t = dot_nt(eye, basis).astype(jnp.bfloat16)
    bt_v[...] = basis_t
    gb_v[...] = dot(basis_t, basis).astype(jnp.bfloat16)
    for t in range(tiles):
        sup_v[t] = sup_ref[:, t * per : (t + 1) * per].astype(jnp.float32)
    acc[...] = jnp.zeros_like(acc)

    @pl.when(me == 0)
    def _():
        ab_v[:, :BLOCK] = jnp.zeros((comps, BLOCK), jnp.bfloat16)

    @pl.when(me == n - 1)
    def _():
        ab_v[:, BLOCK + pixels :] = jnp.zeros((comps, BLOCK), jnp.bfloat16)

    load_ab(0).wait()
    load_ab(1).wait()

    def tile(t):
        load_sp(t).wait()
        for c in range(TILE // CHUNK):
            at = pl.multiple_of(t * TILE + c * CHUNK, CHUNK)
            project = dot(bt_v[...], sp_v[:, pl.ds(at, CHUNK)])
            image = dot(gb_v[...], ab_v[:, pl.ds(pl.multiple_of(at + BLOCK, BLOCK), CHUNK)])
            for r in range(0, comps, ROWS):
                wide = ab_v[r : r + ROWS, pl.ds(at, CHUNK + 2 * BLOCK)].astype(jnp.float32)
                width = CHUNK + 2 * BLOCK
                low = pltpu.roll(wide, 1, 1)[:, BLOCK : BLOCK + CHUNK]
                high = pltpu.roll(wide, width - 1, 1)[:, BLOCK : BLOCK + CHUNK]
                centre = wide[:, BLOCK : BLOCK + CHUNK]
                first = c * CHUNK // BLOCK
                active = jnp.concatenate(
                    [
                        jnp.broadcast_to(sup_v[t, r : r + ROWS, k : k + 1], (ROWS, BLOCK))
                        for k in range(first, first + CHUNK // BLOCK)
                    ],
                    axis=1,
                )
                under = image[r : r + ROWS] + (2.0 * smooth_weight * centre + sparsity)
                over = (active * centre) * (project[r : r + ROWS] + smooth_weight * (low + high))
                inv = pl.reciprocal(under, approx=True)
                inv = inv * (2.0 - under * inv)
                an_v[r : r + ROWS, pl.ds(at, CHUNK)] = (over * inv).astype(jnp.bfloat16)
        where = pl.ds(pl.multiple_of(t * TILE, TILE), TILE)
        fresh = an_v[:, where]
        acc[:, :bands] += dot_nt(fresh, sp_v[:, where])
        acc[:, gram_at:] += dot_nt(fresh, fresh)
        store_an(t).start()

    def inner(t, carry):
        load_ab(t + 1).wait()
        tile(t)
        return carry

    pl.semaphore_wait(barrier, n - 1)

    @pl.when(me < n - 1)
    def _():
        to_right.start()

    @pl.when(me > 0)
    def _():
        to_left.start()

    lax.fori_loop(1, tiles - 1, inner, 0)

    @pl.when(me > 0)
    def _():
        to_right.wait_recv()
        to_left.wait_send()

    @pl.when(me < n - 1)
    def _():
        to_left.wait_recv()
        to_right.wait_send()

    def outer(j, carry):
        tile((1 - j) * (tiles - 1))
        return carry

    lax.fori_loop(0, 2, outer, 0)

    mine = pl.multiple_of(core * half, half)
    theirs = pl.multiple_of((1 - core) * half, half)
    swap = pltpu.make_async_remote_copy(
        src_ref=acc.at[pl.ds(theirs, half)], dst_ref=half_in,
        send_sem=half_s, recv_sem=half_r,
        device_id={"depth": partner}, device_id_type=pl.DeviceIdType.MESH,
    )
    swap.start()
    swap.wait()
    summed = acc[pl.ds(mine, half), :] + half_in[...]
    half_in[...] = summed
    def split(x):
        high = x.astype(jnp.bfloat16)
        return high, x - high.astype(jnp.float32)

    whole = bands // BLOCK * BLOCK
    tail = bands - whole
    high, low = split(summed[:, :whole])
    tail_high, tail_low = split(summed[:, whole:gram_at])
    send_v[:, :comps] = summed[:, gram_at:].astype(jnp.bfloat16)
    send_v[:, comps : comps + whole] = high
    send_v[:, comps + whole : comps + 2 * whole] = low.astype(jnp.bfloat16)
    send_v[:, comps + 2 * whole :] = (tail_high.astype(jnp.float32) + pltpu.roll(tail_low, tail, 1)).astype(jnp.bfloat16)

    owner = lax.rem(chip, stride) == 0
    home = lax.div(chip, stride)

    def give(off):
        w = lax.rem(home + off, owners)
        return w * stride, pltpu.make_async_remote_copy(
            src_ref=send_v.at[pl.ds(pl.multiple_of(w * rows, rows), rows)], dst_ref=recv_v.at[chip],
            send_sem=red_s.at[off], recv_sem=red_r.at[chip],
            device_id={"depth": 2 * w * stride + core}, device_id_type=pl.DeviceIdType.MESH,
        )

    def take(s):
        return pltpu.make_async_remote_copy(
            src_ref=send_v.at[pl.ds(0, rows)], dst_ref=recv_v.at[s],
            send_sem=red_s.at[0], recv_sem=red_r.at[s],
            device_id={"depth": partner}, device_id_type=pl.DeviceIdType.MESH,
        )

    for off in range(owners):
        dest, copy = give(off)
        pl.when(dest != chip)(copy.start)

    my_row = pl.multiple_of(home * rows, rows)
    out_row = pl.multiple_of(mine + my_row, rows)

    def spread(off, at, src):
        return pltpu.make_async_remote_copy(
            src_ref=back_v.at[pl.ds(at, rows)], dst_ref=back_v.at[pl.ds(at, rows)],
            send_sem=gat_s.at[off], recv_sem=gat_r.at[src],
            device_id={"depth": 2 * lax.rem(chip + off, chips) + core}, device_id_type=pl.DeviceIdType.MESH,
        )

    @pl.when(owner)
    def _():
        recv_v[chip] = jnp.zeros(recv_v.shape[1:], recv_v.dtype)
        for s in range(chips):
            pl.when(s != chip)(take(s).wait_recv)
        own = half_in[pl.ds(my_row, rows), :]
        total = recv_v[0].astype(jnp.float32)
        for s in range(1, chips):
            total = total + recv_v[s].astype(jnp.float32)
        gram_high, gram_low = split(own[:, gram_at:] + total[:, :comps])
        lower = dot(gram_high, bt_v[...]) + dot(gram_low.astype(jnp.bfloat16), bt_v[...])
        ends = total[:, comps + 2 * whole :]
        ends = ends + pltpu.roll(ends, BLOCK - tail, 1)
        middle = total[:, comps : comps + whole] + total[:, comps + whole : comps + 2 * whole]
        cross = own[:, :bands] + jnp.concatenate([middle, ends], axis=1)[:, :bands]
        mine_t = bt_v[pl.ds(out_row, rows), :].astype(jnp.float32)
        back_v[pl.ds(out_row, rows), :bands] = (mine_t * cross / lower).astype(jnp.bfloat16)
        for off in range(1, chips):
            spread(off, out_row, home).start()

    for w in range(owners):
        at = pl.multiple_of(mine + w * rows, rows)
        pl.when(chip != w * stride)(spread(0, at, w).wait_recv)

    forward = pltpu.make_async_remote_copy(
        src_ref=back_v.at[pl.ds(mine, half)], dst_ref=back_v.at[pl.ds(mine, half)],
        send_sem=fwd_s, recv_sem=fwd_r,
        device_id={"depth": partner}, device_id_type=pl.DeviceIdType.MESH,
    )
    forward.start()

    for off in range(owners):
        dest, copy = give(off)
        pl.when(dest != chip)(copy.wait_send)

    @pl.when(owner)
    def _():
        for off in range(1, chips):
            spread(off, out_row, home).wait_send()

    for t in range(tiles):
        store_an(t).wait()
    forward.wait()
    bn_ref[...] = back_v[:, :bands]


def local(spectra, basis, abundance, support):
    n = lax.axis_size("depth")
    bands, pixels = spectra.shape
    comps = abundance.shape[0]
    chips = n // 2
    owners = min(chips, 8)
    tiles = pixels // TILE
    padded = -(-bands // BLOCK) * BLOCK
    lanes = padded + comps
    sent = comps + 2 * (bands // BLOCK * BLOCK) + BLOCK
    half = comps // 2
    dma = pltpu.SemaphoreType.DMA
    macs = comps * (2 * bands + 2 * comps) * pixels
    bn_t, abundance_next = pl.pallas_call(
        functools.partial(kernel, n),
        out_shape=(
            jax.ShapeDtypeStruct((comps, bands), jnp.bfloat16),
            jax.ShapeDtypeStruct((comps, pixels), jnp.bfloat16),
        ),
        in_specs=[
            pl.BlockSpec(memory_space=pl.ANY),
            pl.BlockSpec(memory_space=pltpu.VMEM),
            pl.BlockSpec(memory_space=pl.ANY),
            pl.BlockSpec(memory_space=pltpu.VMEM),
        ],
        out_specs=(pl.BlockSpec(memory_space=pltpu.VMEM), pl.BlockSpec(memory_space=pl.ANY)),
        scratch_shapes=[
            pltpu.VMEM((bands, pixels), jnp.bfloat16),
            pltpu.VMEM((comps, pixels + 2 * BLOCK), jnp.bfloat16),
            pltpu.VMEM((comps, pixels), jnp.bfloat16),
            pltpu.VMEM((tiles, comps, TILE // BLOCK), jnp.float32),
            pltpu.VMEM((comps, bands), jnp.bfloat16),
            pltpu.VMEM((comps, comps), jnp.bfloat16),
            pltpu.VMEM((comps, lanes), jnp.float32),
            pltpu.VMEM((half, lanes), jnp.float32),
            pltpu.VMEM((half, sent), jnp.bfloat16),
            pltpu.VMEM((chips, half // owners, sent), jnp.bfloat16),
            pltpu.VMEM((comps, padded), jnp.bfloat16),
            dma((tiles,)), dma((tiles,)), dma((tiles,)),
            dma((2,)), dma((2,)), dma, dma,
            dma((owners,)), dma((chips,)),
            dma((chips,)), dma((owners,)),
            dma, dma,
        ],
        compiler_params=pltpu.CompilerParams(
            collective_id=0, has_side_effects=True, vmem_limit_bytes=48 * 1024 * 1024
        ),
        cost_estimate=pl.CostEstimate(
            flops=2 * macs, bytes_accessed=2 * pixels * (bands + 2 * comps), transcendentals=0
        ),
    )(spectra, basis, abundance, support)
    return bn_t.T, abundance_next


def solution(mesh):
    placed = (
        P(None, ("holes", "depth")),
        P(),
        P(None, ("holes", "depth")),
        P(None, ("holes", "depth")),
    )
    return jax.shard_map(
        local,
        mesh=mesh,
        in_specs=placed,
        out_specs=(P("holes", None), P(None, ("holes", "depth"))),
        check_vma=False,
    )
```

time: 163 us -> 45.6 us (0.28)
  waiting for transfers between devices: 95.5 us -> 0 us
  matrix products: 43.3 us -> 0 us
  Pallas kernels: 0 us -> 35.5 us
  between operations: 14.1 us -> 0.66 us
  starting transfers between devices: 3.82 us -> 0 us
  local copies, waits for them, and re-layouts: 5.63 us -> 9.19 us
    psum x1 -> x0, waiting for transfers between devices: 95.5 us -> none  [local(): cross_all, gram_all = lax.psum((cross, gram_abund), 'depth')]
    dot_general x5 -> x0, matrix products: 43.3 us -> none  [the longest x1 23.2 us: local(): image = jnp.dot(gram_basis, abundance, preferred_element_type=jnp.float32)]
    pallas_call x0 -> x1, Pallas kernels: none -> 35.5 us  [local(): pl.pallas_call(functools.partial(kernel, n), out_shape=(jax.ShapeDtypeStr...]
    unnamed x6 -> x7, local copies, waits for them, and re-layouts: 0.01 us -> 9.19 us
    broadcast_in_dim x1 -> x0, local copies, waits for them, and re-layouts: 4.56 us -> none  [local(): active = jnp.repeat(support.astype(jnp.float32), BLOCK, axis=1)]
    ppermute x2 -> x0, starting transfers between devices: 3.78 us -> none  [the longest x1 2.36 us: extended(): lax.ppermute(lax.slice_in_dim(block, block.shape[dim] - width, None, axis...]
  transfers between devices with their start and end apart: 3 -> 0, of which waited for: 1 -> 0; matrix products, arithmetic and copies ran while one was open for 5% -> 0% of each run, Pallas kernels for 0% -> 0%
where the time goes in v1:
time: 45.6 us; the launch traced here: 45.3 us
  Pallas kernels  35.5 us (78%)
  local copies, waits for them, and re-layouts  9.19 us (20%)
  between operations  0.66 us (1%)
    pallas_call x1, Pallas kernels, local(): pl.pallas_call(functools.partial(kernel, n), out_shape=(jax.ShapeDtypeStr...  35.5 us
    unnamed x7, local copies, waits for them, and re-layouts  9.19 us

profile of v1, /device:TPU:0, one launch (start us, length us, event | category | flops | bytes accessed | tf_op | source)
XLA Modules:
  0.0 45.3 jit_solution(16520367145984790637)
XLA Ops:
  0.6 0.9 %copy.6.sup_ref = s32[256,64]{1,0:T(8,128)S(1)} copy(s32[256,64]{0,1:T(8,128)} %param.7) | data formatting | bytes 131072 | tf_op args[3]
  1.6 0.0 copy-start.1
  1.6 0.9 %copy-done.1 = bf16[288,256]{1,0:T(8,128)(2,1)S(1)} copy-done((bf16[288,256]{1,0:T(8,128)(2,1)S(1)}, bf16[288,256]{1,0:T(8,128)(2,1)}, u32[]{:S(2)}) %copy-start.1) | copy-done | bytes 147480
  2.5 35.5 %shard_map.59 = (bf16[256,288]{1,0:T(8,128)(2,1)S(1)}, bf16[256,8192]{1,0:T(8,128)(2,1)S(1)}) custom-call(bf16[288,8192]{1,0:T(8,128)(2,1)} %sp_hbm.1, bf16[288,256]{1,0:T(8,128)(2,1)S(1)} %copy-done.1, bf16[256,8192]{1,0:T(8,128)(2,1)} %ab_hbm.1, s32[256,64]{1,0:T(8,128)S(1)} %copy.6.sup_ref), custom_call_target="tpu_custom_call" | custom-call | flops 4563402752 | bytes 13107200 | tf_op jit(solution)/shard_map/pallas_call | solution.py:290
  38.0 0.0 copy-start
  38.0 1.9 %copy-done = bf16[256,8192]{1,0:T(8,128)(2,1)} copy-done((bf16[256,8192]{1,0:T(8,128)(2,1)}, bf16[256,8192]{1,0:T(8,128)(2,1)S(1)}, u32[]{:S(2)}) %copy-start) | copy-done | bytes 4194328
  39.9 0.8 %copy.7 = bf16[288,256]{1,0:T(8,128)(2,1)} copy(bf16[288,256]{0,1:T(8,128)(2,1)S(1)} %bitcast.1) | data formatting | bytes 294912
  40.7 4.6 %copy.9 = bf16[256,8192]{1,0:T(8,128)(2,1)} copy(bf16[256,8192]{1,0:T(8,128)(2,1)} %copy-done) | data formatting | bytes 8388608
Async XLA Ops:
  1.6 0.9 %copy-start.1 = (bf16[288,256]{1,0:T(8,128)(2,1)S(1)}, bf16[288,256]{1,0:T(8,128)(2,1)}, u32[]{:S(2)}) copy-start(bf16[288,256]{1,0:T(8,128)(2,1)} %basis_ref.1) | copy-start | bytes 442372
  38.0 1.9 %copy-start = (bf16[256,8192]{1,0:T(8,128)(2,1)}, bf16[256,8192]{1,0:T(8,128)(2,1)S(1)}, u32[]{:S(2)}) copy-start(bf16[256,8192]{1,0:T(8,128)(2,1)S(1)} %get-tuple-element.11) | copy-start | bytes 12582916

commit v2 on v1

--- a/solution.py
+++ b/solution.py
@@ -11,6 +11,7 @@
 TILE = 1024
 CHUNK = 256
 ROWS = 64
+PIECES = 8
 NT = (((1,), (1,)), ((), ()))
 
 smooth_weight = 3000.0
@@ -26,9 +27,9 @@
 
 
 def kernel(
-    n, sp_hbm, basis_ref, ab_hbm, sup_ref, bn_ref, an_hbm,
-    sp_v, ab_v, an_v, sup_v, bt_v, gb_v, acc, half_in, send_v, recv_v, back_v,
-    sp_sem, ab_sem, an_sem, halo_s, halo_r, half_s, half_r, red_s, red_r, gat_s, gat_r, fwd_s, fwd_r,
+    n, sp_hbm, basis_hbm, ab_hbm, sup_hbm, bn_ref, an_hbm,
+    sp_v, ab_v, an_v, basis_v, flags_v, sup_v, bt_v, gb_v, acc, half_in, send_v, recv_v, back_v,
+    small_sem, sp_sem, ab_sem, an_sem, halo_s, halo_r, half_s, half_r, red_s, red_r, gat_s, gat_r,
 ):
     bands, pixels = sp_hbm.shape
     comps = ab_hbm.shape[0]
@@ -61,6 +62,10 @@
         where = pl.ds(pl.multiple_of(t * TILE, TILE), TILE)
         return pltpu.make_async_copy(an_v.at[:, where], an_hbm.at[:, where], an_sem.at[t])
 
+    load_basis = pltpu.make_async_copy(basis_hbm, basis_v, small_sem.at[0])
+    load_flags = pltpu.make_async_copy(sup_hbm, flags_v, small_sem.at[1])
+    load_basis.start()
+    load_flags.start()
     load_ab(0).start()
     load_ab(1).start()
     load_sp(1).start()
@@ -86,16 +91,19 @@
         device_id={"depth": lax.rem(me + n - 1, n)}, device_id_type=pl.DeviceIdType.MESH,
     )
 
-    basis = basis_ref[...]
+    acc[...] = jnp.zeros_like(acc)
+    load_basis.wait()
+    basis = basis_v[...]
     eye = (
         lax.broadcasted_iota(jnp.int32, (comps, comps), 0) == lax.broadcasted_iota(jnp.int32, (comps, comps), 1)
     ).astype(jnp.bfloat16)
     basis_t = dot_nt(eye, basis).astype(jnp.bfloat16)
     bt_v[...] = basis_t
     gb_v[...] = dot(basis_t, basis).astype(jnp.bfloat16)
+    load_flags.wait()
+    flags = dot_nt(eye, flags_v[...].astype(jnp.float32).astype(jnp.bfloat16))
     for t in range(tiles):
-        sup_v[t] = sup_ref[:, t * per : (t + 1) * per].astype(jnp.float32)
-    acc[...] = jnp.zeros_like(acc)
+        sup_v[t] = flags[:, t * per : (t + 1) * per]
 
     @pl.when(me == 0)
     def _():
@@ -221,11 +229,11 @@
     my_row = pl.multiple_of(home * rows, rows)
     out_row = pl.multiple_of(mine + my_row, rows)
 
-    def spread(off, at, src):
+    def spread(off, at):
         return pltpu.make_async_remote_copy(
             src_ref=back_v.at[pl.ds(at, rows)], dst_ref=back_v.at[pl.ds(at, rows)],
-            send_sem=gat_s.at[off], recv_sem=gat_r.at[src],
-            device_id={"depth": 2 * lax.rem(chip + off, chips) + core}, device_id_type=pl.DeviceIdType.MESH,
+            send_sem=gat_s.at[off], recv_sem=gat_r.at[lax.div(at, rows)],
+            device_id={"depth": lax.rem(me + off, n)}, device_id_type=pl.DeviceIdType.MESH,
         )
 
     @pl.when(owner)
@@ -245,19 +253,8 @@
         cross = own[:, :bands] + jnp.concatenate([middle, ends], axis=1)[:, :bands]
         mine_t = bt_v[pl.ds(out_row, rows), :].astype(jnp.float32)
         back_v[pl.ds(out_row, rows), :bands] = (mine_t * cross / lower).astype(jnp.bfloat16)
-        for off in range(1, chips):
-            spread(off, out_row, home).start()
-
-    for w in range(owners):
-        at = pl.multiple_of(mine + w * rows, rows)
-        pl.when(chip != w * stride)(spread(0, at, w).wait_recv)
-
-    forward = pltpu.make_async_remote_copy(
-        src_ref=back_v.at[pl.ds(mine, half)], dst_ref=back_v.at[pl.ds(mine, half)],
-        send_sem=fwd_s, recv_sem=fwd_r,
-        device_id={"depth": partner}, device_id_type=pl.DeviceIdType.MESH,
-    )
-    forward.start()
+        for off in range(1, n):
+            spread(off, out_row).start()
 
     for off in range(owners):
         dest, copy = give(off)
@@ -265,13 +262,35 @@
 
     @pl.when(owner)
     def _():
-        for off in range(1, chips):
-            spread(off, out_row, home).wait_send()
+        for off in range(1, n):
+            spread(off, out_row).wait_send()
 
     for t in range(tiles):
         store_an(t).wait()
-    forward.wait()
+    for w in range(2 * owners):
+        at = w * rows
+        source = 2 * (w % owners) * stride + w // owners
+        pl.when(me != source)(spread(0, at).wait_recv)
     bn_ref[...] = back_v[:, :bands]
+
+
+def settle(bn_t_ref, an_in, bn_ref, an_out, sem):
+    comps = an_in.shape[0]
+    rows = comps // PIECES
+    copies = [
+        pltpu.make_async_copy(an_in.at[pl.ds(i * rows, rows)], an_out.at[pl.ds(i * rows, rows)], sem.at[i])
+        for i in range(PIECES)
+    ]
+    for copy in copies:
+        copy.start()
+    eye = (
+        lax.broadcasted_iota(jnp.int32, (comps, comps), 0) == lax.broadcasted_iota(jnp.int32, (comps, comps), 1)
+    ).astype(jnp.bfloat16)
+    bn_ref[...] = lax.dot_general(
+        bn_t_ref[...], eye, (((0,), (0,)), ((), ())), preferred_element_type=jnp.float32
+    ).astype(jnp.bfloat16)
+    for copy in copies:
+        copy.wait()
 
 
 def local(spectra, basis, abundance, support):
@@ -295,15 +314,17 @@
         ),
         in_specs=[
             pl.BlockSpec(memory_space=pl.ANY),
-            pl.BlockSpec(memory_space=pltpu.VMEM),
+            pl.BlockSpec(memory_space=pltpu.HBM),
             pl.BlockSpec(memory_space=pl.ANY),
-            pl.BlockSpec(memory_space=pltpu.VMEM),
+            pl.BlockSpec(memory_space=pltpu.HBM),
         ],
         out_specs=(pl.BlockSpec(memory_space=pltpu.VMEM), pl.BlockSpec(memory_space=pl.ANY)),
         scratch_shapes=[
             pltpu.VMEM((bands, pixels), jnp.bfloat16),
             pltpu.VMEM((comps, pixels + 2 * BLOCK), jnp.bfloat16),
             pltpu.VMEM((comps, pixels), jnp.bfloat16),
+            pltpu.VMEM(basis.shape, jnp.bfloat16),
+            pltpu.VMEM(support.shape[::-1], jnp.int32),
             pltpu.VMEM((tiles, comps, TILE // BLOCK), jnp.float32),
             pltpu.VMEM((comps, bands), jnp.bfloat16),
             pltpu.VMEM((comps, comps), jnp.bfloat16),
@@ -312,11 +333,10 @@
             pltpu.VMEM((half, sent), jnp.bfloat16),
             pltpu.VMEM((chips, half // owners, sent), jnp.bfloat16),
             pltpu.VMEM((comps, padded), jnp.bfloat16),
-            dma((tiles,)), dma((tiles,)), dma((tiles,)),
+            dma((2,)), dma((tiles,)), dma((tiles,)), dma((tiles,)),
             dma((2,)), dma((2,)), dma, dma,
             dma((owners,)), dma((chips,)),
-            dma((chips,)), dma((owners,)),
-            dma, dma,
+            dma((n,)), dma((2 * owners,)),
         ],
         compiler_params=pltpu.CompilerParams(
             collective_id=0, has_side_effects=True, vmem_limit_bytes=48 * 1024 * 1024
@@ -324,8 +344,18 @@
         cost_estimate=pl.CostEstimate(
             flops=2 * macs, bytes_accessed=2 * pixels * (bands + 2 * comps), transcendentals=0
         ),
-    )(spectra, basis, abundance, support)
-    return bn_t.T, abundance_next
+    )(spectra, basis, abundance, support.T)
+    return pl.pallas_call(
+        settle,
+        out_shape=(
+            jax.ShapeDtypeStruct((bands, comps), jnp.bfloat16),
+            jax.ShapeDtypeStruct((comps, pixels), jnp.bfloat16),
+        ),
+        in_specs=[pl.BlockSpec(memory_space=pltpu.VMEM), pl.BlockSpec(memory_space=pl.ANY)],
+        out_specs=(pl.BlockSpec(memory_space=pltpu.VMEM), pl.BlockSpec(memory_space=pl.ANY)),
+        scratch_shapes=[dma((PIECES,))],
+        compiler_params=pltpu.CompilerParams(vmem_limit_bytes=4 * 1024 * 1024),
+    )(bn_t, abundance_next)
 
 
 def solution(mesh):

time: 45.6 us -> 40.3 us (0.88)
  local copies, waits for them, and re-layouts: 9.19 us -> 1.74 us
  Pallas kernels: 35.5 us -> 37.7 us
    unnamed x7 -> x4, local copies, waits for them, and re-layouts: 9.19 us -> 1.74 us
    pallas_call x0 -> x1, Pallas kernels: none -> 2.76 us  [local(): pl.pallas_call(settle, out_shape=(jax.ShapeDtypeStruct((bands, comps), jn...]
    pallas_call x1, Pallas kernels: 35.5 us -> 35 us  [local(): pl.pallas_call(functools.partial(kernel, n), out_shape=(jax.ShapeDtypeStr...]
where the time goes in v2:
time: 40.3 us; the launch traced here: 40.1 us
  Pallas kernels  37.7 us (94%)
  local copies, waits for them, and re-layouts  1.74 us (4%)
  between operations  0.65 us (2%)
    pallas_call x1, Pallas kernels, local(): pl.pallas_call(functools.partial(kernel, n), out_shape=(jax.ShapeDtypeStr...  35 us
    pallas_call x1, Pallas kernels, local(): pl.pallas_call(settle, out_shape=(jax.ShapeDtypeStruct((bands, comps), jn...  2.76 us
    unnamed x4, local copies, waits for them, and re-layouts  1.74 us

profile of v2, /device:TPU:0, one launch (start us, length us, event | category | flops | bytes accessed | tf_op | source)
XLA Modules:
  0.0 40.1 jit_solution(179909101139236693)
XLA Ops:
  0.6 0.0 copy-start
  0.6 0.9 %copy-done = bf16[288,256]{1,0:T(8,128)(2,1)S(1)} copy-done((bf16[288,256]{1,0:T(8,128)(2,1)S(1)}, bf16[288,256]{1,0:T(8,128)(2,1)}, u32[]{:S(2)}) %copy-start) | copy-done | bytes 147480
  1.5 0.0 copy-start.1
  1.5 0.8 %copy-done.1 = s32[256,64]{0,1:T(8,128)S(1)} copy-done((s32[256,64]{0,1:T(8,128)S(1)}, s32[256,64]{0,1:T(8,128)}, u32[]{:S(2)}) %copy-start.1) | copy-done | bytes 65560
  2.4 35.0 %shard_map.59 = (bf16[256,288]{1,0:T(8,128)(2,1)S(1)}, bf16[256,8192]{1,0:T(8,128)(2,1)S(1)}) custom-call(bf16[288,8192]{1,0:T(8,128)(2,1)} %sp_hbm.1, bf16[288,256]{1,0:T(8,128)(2,1)S(1)} %copy-done, bf16[256,8192]{1,0:T(8,128)(2,1)} %ab_hbm.1, s32[64,256]{1,0:T(8,128)S(1)} %bitcast.1), custom_call_target="tpu_custom_call" | custom-call | flops 4563402752 | bytes 13107200 | tf_op jit(solution)/shard_map/pallas_call | solution.py:309
  37.4 2.8 %shard_map.60 = (bf16[288,256]{1,0:T(8,128)(2,1)}, bf16[256,8192]{1,0:T(8,128)(2,1)}) custom-call(bf16[256,288]{1,0:T(8,128)(2,1)S(1)} %get-tuple-element.4.bn_t_ref, bf16[256,8192]{1,0:T(8,128)(2,1)S(1)} %get-tuple-element.5.an_in), custom_call_target="tpu_custom_call" | custom-call | tf_op jit(solution)/shard_map/pallas_call | solution.py:348
Async XLA Ops:
  0.6 0.9 %copy-start = (bf16[288,256]{1,0:T(8,128)(2,1)S(1)}, bf16[288,256]{1,0:T(8,128)(2,1)}, u32[]{:S(2)}) copy-start(bf16[288,256]{1,0:T(8,128)(2,1)} %basis_hbm.1) | copy-start | bytes 442372
  1.5 0.8 %copy-start.1 = (s32[256,64]{0,1:T(8,128)S(1)}, s32[256,64]{0,1:T(8,128)}, u32[]{:S(2)}) copy-start(s32[256,64]{0,1:T(8,128)} %param.7) | copy-start | bytes 196612

commit v3 on v2

--- a/solution.py
+++ b/solution.py
@@ -8,8 +8,8 @@
 from jax.sharding import PartitionSpec as P
 
 BLOCK = 128
-TILE = 1024
-CHUNK = 256
+TILE = 2048
+CHUNK = 512
 ROWS = 64
 PIECES = 8
 NT = (((1,), (1,)), ((), ()))

time: 40.3 us -> 39.2 us (0.973)
  Pallas kernels: 37.7 us -> 36.6 us
    pallas_call x1, Pallas kernels: 35 us -> 33.8 us  [local(): pl.pallas_call(functools.partial(kernel, n), out_shape=(jax.ShapeDtypeStr...]
where the time goes in v3:
time: 39.2 us; the launch traced here: 39 us
  Pallas kernels  36.6 us (93%)
  local copies, waits for them, and re-layouts  1.74 us (4%)
  between operations  0.65 us (2%)
    pallas_call x1, Pallas kernels, local(): pl.pallas_call(functools.partial(kernel, n), out_shape=(jax.ShapeDtypeStr...  33.8 us
    pallas_call x1, Pallas kernels, local(): pl.pallas_call(settle, out_shape=(jax.ShapeDtypeStruct((bands, comps), jn...  2.76 us
    unnamed x4, local copies, waits for them, and re-layouts  1.74 us

profile of v3, /device:TPU:0, one launch (start us, length us, event | category | flops | bytes accessed | tf_op | source)
XLA Modules:
  0.0 39.0 jit_solution(3174028710359234278)
XLA Ops:
  0.6 0.0 copy-start
  0.6 0.9 %copy-done = bf16[288,256]{1,0:T(8,128)(2,1)S(1)} copy-done((bf16[288,256]{1,0:T(8,128)(2,1)S(1)}, bf16[288,256]{1,0:T(8,128)(2,1)}, u32[]{:S(2)}) %copy-start) | copy-done | bytes 147480
  1.5 0.0 copy-start.1
  1.5 0.8 %copy-done.1 = s32[256,64]{0,1:T(8,128)S(1)} copy-done((s32[256,64]{0,1:T(8,128)S(1)}, s32[256,64]{0,1:T(8,128)}, u32[]{:S(2)}) %copy-start.1) | copy-done | bytes 65560
  2.4 33.8 %shard_map.59 = (bf16[256,288]{1,0:T(8,128)(2,1)S(1)}, bf16[256,8192]{1,0:T(8,128)(2,1)S(1)}) custom-call(bf16[288,8192]{1,0:T(8,128)(2,1)} %sp_hbm.1, bf16[288,256]{1,0:T(8,128)(2,1)S(1)} %copy-done, bf16[256,8192]{1,0:T(8,128)(2,1)} %ab_hbm.1, s32[64,256]{1,0:T(8,128)S(1)} %bitcast.1), custom_call_target="tpu_custom_call" | custom-call | flops 4563402752 | bytes 13107200 | tf_op jit(solution)/shard_map/pallas_call | solution.py:309
  36.2 2.8 %shard_map.60 = (bf16[288,256]{1,0:T(8,128)(2,1)}, bf16[256,8192]{1,0:T(8,128)(2,1)}) custom-call(bf16[256,288]{1,0:T(8,128)(2,1)S(1)} %get-tuple-element.4.bn_t_ref, bf16[256,8192]{1,0:T(8,128)(2,1)S(1)} %get-tuple-element.5.an_in), custom_call_target="tpu_custom_call" | custom-call | tf_op jit(solution)/shard_map/pallas_call | solution.py:348
Async XLA Ops:
  0.6 0.9 %copy-start = (bf16[288,256]{1,0:T(8,128)(2,1)S(1)}, bf16[288,256]{1,0:T(8,128)(2,1)}, u32[]{:S(2)}) copy-start(bf16[288,256]{1,0:T(8,128)(2,1)} %basis_hbm.1) | copy-start | bytes 442372
  1.5 0.8 %copy-start.1 = (s32[256,64]{0,1:T(8,128)S(1)}, s32[256,64]{0,1:T(8,128)}, u32[]{:S(2)}) copy-start(s32[256,64]{0,1:T(8,128)} %param.7) | copy-start | bytes 196612
